TPU v7x, 32 devices: a whole 2x2x4 slice. The times are simulated.
32 devices in a mesh: tile: 8 (over z, core), tm: 4 (over y, x).
Axes of the slice: x: 2, y: 2, z: 4, core: 2. Of those that a mesh axis runs over, the one named last changes fastest.
Arguments:
- src_snap: bfloat16 [128, 8, 128, 256], P('tile', 'tm'), may hold values from -6 to 6
- rcv_snap: bfloat16 [128, 8, 128, 256], P('tile', 'tm'), may hold values from -6 to 6
- q_rate: float32 [256], replicated, may hold values from 0.05 to 1.5
- nbr_device: int32 [128, 2], replicated, may hold values from 0 to 7, all different within a row; in each aligned block of 16 rows (0 to 15, 16 to 31, ...) at most 5 rows name the same one
- nbr_index: int32 [128, 2], replicated, may hold values from 0 to 15
- depth_extent: int32 [128], P('tile'), may hold values from 16 to 256, as said below
Outputs:
- image: float32 [128, 8, 49, 256], P(('tile', 'tm'))
Inputs may be any that keep to these rules, and one draw needn't show every extreme that they name: `nbr_device`: the two devices of a row differ; among the rows of one device (aligned blocks of 16 rows) no device is named more than 5 times, and in some device's rows one device is named exactly 5 times. Cells of a tile's gathers at depth depth_extent[s] and below are zero.
All inputs are finite; a program needn't handle non-finite values.
Results may differ from a plain program's by a relative error of at most 0.0003.
Values may be sent and summed in bfloat16 or wider, within the bound.
A program may use at most 128 MiB of HBM per device.

v0:
```python
import functools
import math

import jax
import jax.numpy as jnp
from jax import lax
from jax.experimental import pallas as pl
from jax.experimental.pallas import tpu as pltpu
from jax.sharding import PartitionSpec as P

GSTEP = 16
HMAX = 24
GB = 8
OFFS = 49
RIM_L = 16
RIM_R = 17
ROWS = 16
SPAN = 56
MESH = pl.DeviceIdType.MESH


def one_hot(rows, columns, rule):
    row = lax.broadcasted_iota(jnp.int32, (rows, columns), 0)
    column = lax.broadcasted_iota(jnp.int32, (rows, columns), 1)
    return rule(row, column).astype(jnp.float32).astype(jnp.bfloat16)


def pick(matrix, values):
    return jnp.dot(matrix, values, preferred_element_type=jnp.float32)


def kernel(
    sizes,
    send_tab,
    arrive_tab,
    extent_ref,
    rate_ref,
    src_ref,
    rcv_ref,
    out_ref,
    edge_cells,
    a_send,
    a_recv,
    b_send,
    b_recv,
    centre,
    acc,
    edge_sem,
    own_sem,
    main_send_sem,
    main_recv_sem,
    a_send_sem,
    a_recv_sem,
    b_send_sem,
    b_recv_sem,
):
    tiles, steps, width, depth, devices, times, capacity, share = sizes
    pieces = 2 * steps
    fields = (src_ref, rcv_ref)
    me_tile = lax.axis_index("tile")
    me_tm = lax.axis_index("tm")

    def rest(count, me, j):
        return lax.rem(me + j, count)

    edge_copies = []
    for f in range(2):
        for k, first in enumerate((width - ROWS, 0, ROWS)):
            copy = pltpu.make_async_copy(
                fields[f].at[:, :, pl.ds(first, ROWS), :],
                edge_cells.at[f, k],
                edge_sem.at[f * 3 + k],
            )
            copy.start()
            edge_copies.append(copy)
    own_copies = []
    for f in range(2):
        copy = pltpu.make_async_copy(
            fields[f].at[pl.ds(me_tm * share, share)], centre.at[f, me_tm], own_sem.at[f]
        )
        copy.start()
        own_copies.append(copy)

    barrier = pltpu.get_barrier_semaphore()
    for j in range(1, times):
        pl.semaphore_signal(
            barrier, inc=1, device_id=(me_tile, rest(times, me_tm, j)), device_id_type=MESH
        )
    for j in range(1, devices):
        pl.semaphore_signal(
            barrier, inc=1, device_id=(rest(devices, me_tile, j), me_tm), device_id_type=MESH
        )
    pl.semaphore_wait(barrier, times + devices - 2)

    main_copies = []
    for j in range(1, times):
        to = rest(times, me_tm, j)
        for f in range(2):
            copy = pltpu.make_async_remote_copy(
                src_ref=fields[f].at[pl.ds(to * share, share)],
                dst_ref=centre.at[f, me_tm],
                send_sem=main_send_sem.at[j, f],
                recv_sem=main_recv_sem.at[j, f],
                device_id=(me_tile, to),
                device_id_type=MESH,
            )
            copy.start()
            main_copies.append(copy)

    for copy in edge_copies:
        copy.wait()

    a_extra = a_send.shape[1] - capacity * pieces
    compress = one_hot(
        a_extra * ROWS, capacity * pieces * ROWS, lambda row, column: column == row * ROWS
    )

    def pack(to):
        extra = []
        for k in range(capacity):
            index = send_tab[0, to, k]
            side = send_tab[1, to, k]
            for f in range(2):
                first = k * pieces + f * steps
                a_send[to, first : first + steps] = edge_cells[f, side, index]
                extra.append(edge_cells[f, 2, index].reshape(steps * ROWS, depth))
        packed = pick(compress, jnp.concatenate(extra, axis=0))
        a_send[to, capacity * pieces :] = packed.astype(jnp.bfloat16).reshape(
            a_extra, ROWS, depth
        )

    def a_copy(j):
        to = rest(devices, me_tile, j)
        return pltpu.make_async_remote_copy(
            src_ref=a_send.at[to],
            dst_ref=a_recv.at[me_tile],
            send_sem=a_send_sem.at[j],
            recv_sem=a_recv_sem.at[j],
            device_id=(to, me_tm),
            device_id_type=MESH,
        )

    @pl.loop(1, devices)
    def _(j):
        pack(rest(devices, me_tile, j))
        a_copy(j).start()

    pack(me_tile)
    a_recv[me_tile] = a_send[me_tile]

    rate = rate_ref[...]

    def weight(part, t):
        step = (part * steps + t).astype(jnp.float32)
        return jnp.exp(rate * step / (steps * times))

    turn_centre = one_hot(
        width - 8, width, lambda row, column: column == width - ROWS - row
    )
    last = width // GSTEP * GSTEP - HMAX * 2

    def centre_pass(part, fresh):
        @pl.loop(0, share)
        def _(i):
            sums = [None] * GB
            for t in range(steps):
                turned = pick(turn_centre, centre[0, part, i, t]) * weight(part, t)
                straight = centre[1, part, i, t].astype(jnp.float32)
                for g in range(1, GB - 2):
                    back = last - GSTEP * g
                    ahead = GSTEP * (g - 1)
                    product = turned[back : back + SPAN] * straight[ahead : ahead + SPAN]
                    sums[g] = product if sums[g] is None else sums[g] + product
            for g in range(1, GB - 2):
                if fresh:
                    acc[i, g] = sums[g]
                else:
                    acc[i, g] += sums[g]

    for copy in own_copies:
        copy.wait()
    centre_pass(me_tm, True)

    @pl.loop(1, devices)
    def _(j):
        a_copy(j).wait()

    b_rims = 2 * share * steps * 2
    b_extra = b_send.shape[1] - b_rims

    def unpack(to):
        packed = None
        for i in range(share):
            tile = to * share + i
            for side in range(2):
                source = arrive_tab[0, 2 * tile + side]
                rank = arrive_tab[1, 2 * tile + side]
                rim = a_recv[source, pl.ds(rank * pieces, pieces)]
                for f in range(2):
                    for t in range(steps):
                        b_send[to, ((f * share + i) * steps + t) * 2 + side] = rim[f * steps + t]
            extra = a_recv[source, capacity * pieces :].reshape(a_extra * ROWS, depth)
            choose = one_hot(
                b_extra * ROWS,
                a_extra * ROWS,
                lambda row, column: (row >= i * pieces)
                & (row < (i + 1) * pieces)
                & (column == rank * pieces + row - i * pieces),
            )
            chosen = pick(choose, extra)
            packed = chosen if packed is None else packed + chosen
        b_send[to, b_rims:] = packed.astype(jnp.bfloat16).reshape(b_extra, ROWS, depth)

    def b_copy(j):
        to = rest(times, me_tm, j)
        return pltpu.make_async_remote_copy(
            src_ref=b_send.at[to],
            dst_ref=b_recv.at[me_tm],
            send_sem=b_send_sem.at[j],
            recv_sem=b_recv_sem.at[j],
            device_id=(me_tile, to),
            device_id_type=MESH,
        )

    @pl.loop(1, times)
    def _(j):
        unpack(rest(times, me_tm, j))
        b_copy(j).start()

    unpack(me_tm)
    b_recv[me_tm] = b_send[me_tm]

    def finish(gathers):
        @pl.loop(0, share)
        def _(i):
            extent = extent_ref[me_tm * share + i]
            cell = lax.broadcasted_iota(jnp.int32, (1, depth), 1)
            mask = (cell < extent).astype(jnp.float32)
            for g in gathers:
                out_ref[i, g] = (
                    acc[i, g][:OFFS] * (1.0 / math.sqrt(steps * times)) * mask
                )

    turn_first = one_hot(SPAN, 4 * ROWS, lambda row, column: column == OFFS - 1 - row)
    turn_last = one_hot(SPAN + ROWS, 4 * ROWS, lambda row, column: column == 4 * ROWS - row)
    wide = width - 3 * ROWS

    def edge_pass(part, fresh):
        @pl.loop(0, share)
        def _(i):
            extra = b_recv[part, b_rims:].reshape(b_extra * ROWS, depth)
            sums = [None] * 3
            for t in range(steps):
                scale = weight(part, t)
                place = i * pieces + t
                rims = (i * steps + t) * 2
                rims_rcv = ((share + i) * steps + t) * 2
                src_left = b_recv[part, rims]
                src_right = b_recv[part, rims + 1]
                rcv_left = b_recv[part, rims_rcv]
                rcv_right = b_recv[part, rims_rcv + 1]
                turned = pick(
                    turn_first,
                    jnp.concatenate([src_left, centre[0, part, i, t, : 3 * ROWS]], axis=0),
                )
                straight = jnp.concatenate(
                    [rcv_left, centre[1, part, i, t, : 3 * ROWS]], axis=0
                ).astype(jnp.float32)
                products = [turned * scale * straight[:SPAN]]
                turn_extra = one_hot(
                    SPAN + ROWS,
                    b_extra * ROWS,
                    lambda row, column: (row == 0) & (column == place),
                )
                turned = pick(
                    turn_last,
                    jnp.concatenate([centre[0, part, i, t, wide:], src_right], axis=0),
                ) + pick(turn_extra, extra)
                turned = turned * scale
                rcv_extra = pick(
                    one_hot(
                        8,
                        b_extra * ROWS,
                        lambda row, column: (row == 0) & (column == place + steps),
                    ),
                    extra,
                )
                straight = jnp.concatenate(
                    [
                        centre[1, part, i, t, wide:].astype(jnp.float32),
                        rcv_right.astype(jnp.float32),
                        rcv_extra,
                    ],
                    axis=0,
                )
                products.append(turned[ROWS:] * straight[:SPAN])
                products.append(turned[:SPAN] * straight[ROWS:])
                sums = [
                    product if total is None else total + product
                    for total, product in zip(sums, products)
                ]
            for g, total in zip((0, GB - 2, GB - 1), sums):
                if fresh:
                    acc[i, g] = total
                else:
                    acc[i, g] += total

    edge_pass(me_tm, True)
    for j in range(1, times):
        for f in range(2):
            main_copies[2 * (j - 1) + f].wait_recv()
        centre_pass(rest(times, me_tm, times - j), False)
    finish(range(1, GB - 2))
    for j in range(1, times):
        b_copy(j).wait_recv()
        edge_pass(rest(times, me_tm, times - j), False)
    finish((0, GB - 2, GB - 1))

    for copy in main_copies:
        copy.wait_send()
    for j in range(1, times):
        b_copy(j).wait_send()


def routes(nbr_device, nbr_index, devices, capacity, tiles):
    own = lax.axis_index("tile")
    count = 2 * tiles
    device = nbr_device.reshape(devices, count)
    index = nbr_index.reshape(devices, count)
    ids = jnp.arange(count, dtype=jnp.int32)
    earlier = ids[None, :] < ids[:, None]
    same = (device[:, :, None] == device[:, None, :]) & earlier[None]
    rank = jnp.sum(same.astype(jnp.int32), axis=2)
    slot = jnp.arange(capacity, dtype=jnp.int32)
    hit = ((device == own)[:, None, :] & (rank[:, None, :] == slot[None, :, None])).astype(jnp.int32)
    wanted = jnp.stack([index, jnp.broadcast_to((ids % 2)[None, :], index.shape)])
    send_tab = jnp.sum(hit[None] * wanted[:, :, None, :], axis=3)
    arrive = jnp.stack([device, rank])
    arrive_tab = lax.dynamic_slice_in_dim(arrive, own, 1, 1)[:, 0]
    return send_tab, arrive_tab


def local(src_snap, rcv_snap, q_rate, nbr_device, nbr_index, depth_extent):
    tiles, steps, width, depth = src_snap.shape
    devices = lax.axis_size("tile")
    times = lax.axis_size("tm")
    capacity = (2 * tiles + devices - 1) // devices + 1
    share = tiles // times
    send_tab, arrive_tab = routes(nbr_device, nbr_index, devices, capacity, tiles)
    pieces = 2 * steps
    a_blocks = capacity * pieces + -(-capacity * pieces // ROWS)
    b_blocks = 2 * share * steps * 2 + -(-share * pieces // ROWS)
    sizes = (tiles, steps, width, depth, devices, times, capacity, share)
    half = jnp.bfloat16
    products = share * GB * OFFS * depth * steps * times
    return pl.pallas_call(
        functools.partial(kernel, sizes),
        out_shape=jax.ShapeDtypeStruct((share, GB, OFFS, depth), jnp.float32),
        in_specs=[pl.BlockSpec(memory_space=pltpu.SMEM)] * 3
        + [pl.BlockSpec(memory_space=pltpu.VMEM)]
        + [pl.BlockSpec(memory_space=pl.ANY)] * 2,
        out_specs=pl.BlockSpec(memory_space=pltpu.VMEM),
        scratch_shapes=[
            pltpu.VMEM((2, 3, tiles, steps, ROWS, depth), half),
            pltpu.VMEM((devices, a_blocks, ROWS, depth), half),
            pltpu.VMEM((devices, a_blocks, ROWS, depth), half),
            pltpu.VMEM((times, b_blocks, ROWS, depth), half),
            pltpu.VMEM((times, b_blocks, ROWS, depth), half),
            pltpu.VMEM((2, times, share, steps, width, depth), half),
            pltpu.VMEM((share, GB, SPAN, depth), jnp.float32),
            pltpu.SemaphoreType.DMA((6,)),
            pltpu.SemaphoreType.DMA((2,)),
            pltpu.SemaphoreType.DMA((times, 2)),
            pltpu.SemaphoreType.DMA((times, 2)),
            pltpu.SemaphoreType.DMA((devices,)),
            pltpu.SemaphoreType.DMA((devices,)),
            pltpu.SemaphoreType.DMA((times,)),
            pltpu.SemaphoreType.DMA((times,)),
        ],
        compiler_params=pltpu.CompilerParams(
            collective_id=0, has_side_effects=True, vmem_limit_bytes=40 * 1024 * 1024
        ),
        cost_estimate=pl.CostEstimate(
            flops=3 * products, bytes_accessed=4 * tiles * steps * width * depth, transcendentals=0
        ),
    )(send_tab, arrive_tab, depth_extent, q_rate.reshape(1, depth), src_snap, rcv_snap)


def pair_kernel(
    sizes,
    device_tab,
    index_tab,
    extent_ref,
    rate_ref,
    src_ref,
    rcv_ref,
    out_ref,
    ranks,
    edge_cells,
    a_send,
    a_recv,
    b_own,
    b_send,
    b_recv,
    centre,
    acc,
    pc_send,
    pc_recv,
    pe_send,
    pe_recv,
    edge_sem,
    own_sem,
    main_send_sem,
    main_recv_sem,
    a_send_sem,
    a_recv_sem,
    b_send_sem,
    b_recv_sem,
    p_send_sem,
    p_recv_sem,
):
    tiles, steps, width, depth, devices, times, capacity, share = sizes
    half = share // 2
    pieces = 2 * steps
    fields = (src_ref, rcv_ref)
    me_tile = lax.axis_index("tile")
    me_tm = lax.axis_index("tm")
    low = lax.rem(me_tm, 2)
    high = lax.div(me_tm, 2)
    by_x = high * 2 + 1 - low
    by_y = (1 - high) * 2 + low
    across = (1 - high) * 2 + 1 - low

    owner = (by_y, by_x, me_tm, me_tm)
    partner = (by_x, by_y, by_x, by_y)
    owner_there = (across, across, by_x, by_y)
    offset = (0, half, 0, half)

    def first_tile(owners, w):
        return owners[w] * share + offset[w]

    edge_copies = []
    for f in range(2):
        for k, first in enumerate((width - ROWS, 0, ROWS)):
            copy = pltpu.make_async_copy(
                fields[f].at[:, :, pl.ds(first, ROWS), :],
                edge_cells.at[f, k],
                edge_sem.at[f * 3 + k],
            )
            copy.start()
            edge_copies.append(copy)

    barrier = pltpu.get_barrier_semaphore()
    for to in (by_x, by_y):
        pl.semaphore_signal(barrier, inc=1, device_id=(me_tile, to), device_id_type=MESH)
    for j in range(1, devices):
        pl.semaphore_signal(
            barrier, inc=1, device_id=(lax.rem(me_tile + j, devices), me_tm), device_id_type=MESH
        )
    pl.semaphore_wait(barrier, devices + 1)

    main_copies = []
    for w in range(4):
        copies = []
        for f in range(2):
            copy = pltpu.make_async_remote_copy(
                src_ref=fields[f].at[pl.ds(first_tile(owner_there, w), half)],
                dst_ref=centre.at[f, 1, w],
                send_sem=main_send_sem.at[w, f],
                recv_sem=main_recv_sem.at[w, f],
                device_id=(me_tile, partner[w]),
                device_id_type=MESH,
            )
            copy.start()
            copies.append(copy)
        main_copies.append(copies)
    own_copies = []
    for w in range(4):
        for f in range(2):
            copy = pltpu.make_async_copy(
                fields[f].at[pl.ds(first_tile(owner, w), half)],
                centre.at[f, 0, w],
                own_sem.at[w, f],
            )
            copy.start()
            own_copies.append(copy)

    for copy in edge_copies:
        copy.wait()

    a_extra = a_send.shape[1] - capacity * pieces
    compress = one_hot(
        a_extra * ROWS, capacity * pieces * ROWS, lambda row, column: column == row * ROWS
    )

    def pack(to):
        def scan(row, carry):
            count, codes = carry
            for side in range(2):
                hit = device_tab[side, to * tiles + row] == me_tile
                code = index_tab[side, to * tiles + row] * 2 + side
                codes = tuple(
                    jnp.where(hit & (count == k), code, codes[k]) for k in range(capacity)
                )
                count = count + hit.astype(jnp.int32)
            return count, codes

        zero = jnp.int32(0)
        _, codes = lax.fori_loop(0, tiles, scan, (zero, (zero,) * capacity))
        extra = []
        for k in range(capacity):
            index = lax.div(codes[k], 2)
            side = lax.rem(codes[k], 2)
            for f in range(2):
                first = k * pieces + f * steps
                a_send[to, first : first + steps] = edge_cells[f, side, index]
                extra.append(edge_cells[f, 2, index].reshape(steps * ROWS, depth))
        packed = pick(compress, jnp.concatenate(extra, axis=0))
        a_send[to, capacity * pieces :] = packed.astype(jnp.bfloat16).reshape(
            a_extra, ROWS, depth
        )

    def a_copy(j):
        to = lax.rem(me_tile + j, devices)
        return pltpu.make_async_remote_copy(
            src_ref=a_send.at[to],
            dst_ref=a_recv.at[me_tile],
            send_sem=a_send_sem.at[j],
            recv_sem=a_recv_sem.at[j],
            device_id=(to, me_tm),
            device_id_type=MESH,
        )

    @pl.loop(1, devices)
    def _(j):
        pack(lax.rem(me_tile + j, devices))
        a_copy(j).start()

    pack(me_tile)
    a_recv[me_tile] = a_send[me_tile]

    base = me_tile * tiles

    @pl.loop(0, tiles)
    def _(row):
        mine = [device_tab[side, base + row] for side in range(2)]

        def count(other, sums):
            theirs = [device_tab[side, base + other] for side in range(2)]
            return tuple(
                sums[side]
                + (theirs[0] == mine[side]).astype(jnp.int32)
                + (theirs[1] == mine[side]).astype(jnp.int32)
                for side in range(2)
            )

        found = lax.fori_loop(0, row, count, (jnp.int32(0), jnp.int32(0)))
        for side in range(2):
            ranks[side, row] = jnp.minimum(found[side], capacity - 1)

    rate = rate_ref[...]

    def weight(part, t):
        step = (part * steps + t).astype(jnp.float32)
        return jnp.exp(rate * step / (steps * times))

    inner = range(1, GB - 2)
    outer = (0, GB - 2, GB - 1)
    turn_centre = one_hot(
        width - 8, width, lambda row, column: column == width - ROWS - row
    )
    last = width // GSTEP * GSTEP - HMAX * 2

    def centre_sums(w, p, part, i):
        sums = [None] * GB
        for t in range(steps):
            turned = pick(turn_centre, centre[0, p, w, i, t]) * weight(part, t)
            straight = centre[1, p, w, i, t].astype(jnp.float32)
            for g in inner:
                back = last - GSTEP * g
                ahead = GSTEP * (g - 1)
                product = turned[back : back + SPAN] * straight[ahead : ahead + SPAN]
                sums[g] = product if sums[g] is None else sums[g] + product
        return sums

    turn_first = one_hot(SPAN, 4 * ROWS, lambda row, column: column == OFFS - 1 - row)
    turn_last = one_hot(SPAN + ROWS, 4 * ROWS, lambda row, column: column == 4 * ROWS - row)
    wide = width - 3 * ROWS
    b_rims = 2 * half * steps * 2
    b_extra = b_send.shape[1] - b_rims

    def edge_sums(rims_ref, w, p, part, i):
        extra = rims_ref[w, b_rims:].reshape(b_extra * ROWS, depth)
        sums = [None] * 3
        for t in range(steps):
            scale = weight(part, t)
            place = i * pieces + t
            rims = (i * steps + t) * 2
            rims_rcv = ((half + i) * steps + t) * 2
            turned = pick(
                turn_first,
                jnp.concatenate([rims_ref[w, rims], centre[0, p, w, i, t, : 3 * ROWS]], axis=0),
            )
            straight = jnp.concatenate(
                [rims_ref[w, rims_rcv], centre[1, p, w, i, t, : 3 * ROWS]], axis=0
            ).astype(jnp.float32)
            products = [turned * scale * straight[:SPAN]]
            turn_extra = one_hot(
                SPAN + ROWS,
                b_extra * ROWS,
                lambda row, column: (row == 0) & (column == place),
            )
            turned = pick(
                turn_last,
                jnp.concatenate(
                    [centre[0, p, w, i, t, wide:], rims_ref[w, rims + 1]], axis=0
                ),
            ) + pick(turn_extra, extra)
            turned = turned * scale
            rcv_extra = pick(
                one_hot(
                    8,
                    b_extra * ROWS,
                    lambda row, column: (row == 0) & (column == place + steps),
                ),
                extra,
            )
            straight = jnp.concatenate(
                [
                    centre[1, p, w, i, t, wide:].astype(jnp.float32),
                    rims_ref[w, rims_rcv + 1].astype(jnp.float32),
                    rcv_extra,
                ],
                axis=0,
            )
            products.append(turned[ROWS:] * straight[:SPAN])
            products.append(turned[:SPAN] * straight[ROWS:])
            sums = [
                product if total is None else total + product
                for total, product in zip(sums, products)
            ]
        return sums

    def own_centre(w):
        @pl.loop(0, half)
        def _(i):
            sums = centre_sums(w, 0, me_tm, i)
            for g in inner:
                acc[w, i, g] = sums[g]

    def own_edge(w):
        @pl.loop(0, half)
        def _(i):
            for g, total in zip(outer, edge_sums(b_own, w, 0, me_tm, i)):
                acc[w, i, g] = total

    def far_centre(w):
        for copy in main_copies[w]:
            copy.wait_recv()

        @pl.loop(0, half)
        def _(i):
            sums = centre_sums(w, 1, partner[w], i)
            for k, g in enumerate(inner):
                total = acc[w, i, g] + sums[g]
                if w < 2:
                    pc_send[w, i, OFFS * k : OFFS * (k + 1)] = total[:OFFS]
                else:
                    acc[w, i, g] = total

    def far_edge(w):
        b_copies[w].wait_recv()

        @pl.loop(0, half)
        def _(i):
            sums = edge_sums(b_recv, w, 1, partner[w], i)
            for k, g in enumerate(outer):
                total = acc[w, i, g] + sums[k]
                if w < 2:
                    pe_send[w, i, OFFS * k : OFFS * (k + 1)] = total[:OFFS]
                else:
                    acc[w, i, g] = total

    def partial_copy(w, send, recv, k):
        return pltpu.make_async_remote_copy(
            src_ref=send.at[w],
            dst_ref=recv.at[w],
            send_sem=p_send_sem.at[k, w],
            recv_sem=p_recv_sem.at[k, w],
            device_id=(me_tile, owner[w]),
            device_id_type=MESH,
        )

    def unpack(first, target, w):
        packed = None
        for i in range(half):
            tile = first + i
            for side in range(2):
                source = device_tab[side, base + tile]
                rank = ranks[side, tile]
                rim = a_recv[source, pl.ds(rank * pieces, pieces)]
                for f in range(2):
                    for t in range(steps):
                        target[w, ((f * half + i) * steps + t) * 2 + side] = rim[f * steps + t]
            extra = a_recv[source, capacity * pieces :].reshape(a_extra * ROWS, depth)
            choose = one_hot(
                b_extra * ROWS,
                a_extra * ROWS,
                lambda row, column: (row >= i * pieces)
                & (row < (i + 1) * pieces)
                & (column == rank * pieces + row - i * pieces),
            )
            chosen = pick(choose, extra)
            packed = chosen if packed is None else packed + chosen
        target[w, b_rims:] = packed.astype(jnp.bfloat16).reshape(b_extra, ROWS, depth)

    def finish(w, gathers, recv):
        @pl.loop(0, half)
        def _(i):
            tile = offset[w] + i
            extent = extent_ref[me_tm * share + tile]
            cell = lax.broadcasted_iota(jnp.int32, (1, depth), 1)
            mask = (cell < extent).astype(jnp.float32)
            for k, g in enumerate(gathers):
                total = acc[w, i, g][:OFFS] + recv[w - 2, i, OFFS * k : OFFS * (k + 1)]
                out_ref[tile, g] = total * (1.0 / math.sqrt(steps * times)) * mask

    for copy in own_copies:
        copy.wait()
    for w in range(4):
        own_centre(w)

    pc_copies = []
    for w in range(2):
        far_centre(w)
        copy = partial_copy(w, pc_send, pc_recv, 0)
        copy.start()
        pc_copies.append(copy)

    @pl.loop(1, devices)
    def _(j):
        a_copy(j).wait()

    b_copies = []
    for w in range(4):
        unpack(first_tile(owner_there, w), b_send, w)
        copy = pltpu.make_async_remote_copy(
            src_ref=b_send.at[w],
            dst_ref=b_recv.at[w],
            send_sem=b_send_sem.at[w],
            recv_sem=b_recv_sem.at[w],
            device_id=(me_tile, partner[w]),
            device_id_type=MESH,
        )
        copy.start()
        b_copies.append(copy)
    for w in range(4):
        unpack(first_tile(owner, w), b_own, w)
        own_edge(w)

    pe_copies = []
    for w in range(2):
        far_edge(w)
        copy = partial_copy(w, pe_send, pe_recv, 1)
        copy.start()
        pe_copies.append(copy)
    for w in (2, 3):
        far_centre(w)
    for w in (2, 3):
        far_edge(w)
    for w in (2, 3):
        pc_copies[w - 2].wait_recv()
        finish(w, inner, pc_recv)
    for w in (2, 3):
        pe_copies[w - 2].wait_recv()
        finish(w, outer, pe_recv)

    for copies in main_copies:
        for copy in copies:
            copy.wait_send()
    for copy in b_copies + pc_copies + pe_copies:
        copy.wait_send()


def paired(src_snap, rcv_snap, q_rate, nbr_device, nbr_index, depth_extent):
    tiles, steps, width, depth = src_snap.shape
    devices = lax.axis_size("tile")
    times = lax.axis_size("tm")
    capacity = (2 * tiles + devices - 1) // devices + 1
    share = tiles // times
    half = share // 2
    pieces = 2 * steps
    a_blocks = capacity * pieces + -(-capacity * pieces // ROWS)
    b_blocks = 2 * half * steps * 2 + -(-half * pieces // ROWS)
    inner_rows = -(-(GB - 3) * OFFS // 8) * 8
    outer_rows = -(-3 * OFFS // 8) * 8
    sizes = (tiles, steps, width, depth, devices, times, capacity, share)
    bf16, f32 = jnp.bfloat16, jnp.float32
    products = share * GB * OFFS * depth * steps * times
    return pl.pallas_call(
        functools.partial(pair_kernel, sizes),
        out_shape=jax.ShapeDtypeStruct((share, GB, OFFS, depth), f32),
        in_specs=[pl.BlockSpec(memory_space=pltpu.SMEM)] * 3
        + [pl.BlockSpec(memory_space=pltpu.VMEM)]
        + [pl.BlockSpec(memory_space=pl.ANY)] * 2,
        out_specs=pl.BlockSpec(memory_space=pltpu.VMEM),
        scratch_shapes=[
            pltpu.SMEM((2, tiles), jnp.int32),
            pltpu.VMEM((2, 3, tiles, steps, ROWS, depth), bf16),
            pltpu.VMEM((devices, a_blocks, ROWS, depth), bf16),
            pltpu.VMEM((devices, a_blocks, ROWS, depth), bf16),
            pltpu.VMEM((4, b_blocks, ROWS, depth), bf16),
            pltpu.VMEM((4, b_blocks, ROWS, depth), bf16),
            pltpu.VMEM((4, b_blocks, ROWS, depth), bf16),
            pltpu.VMEM((2, 2, 4, half, steps, width, depth), bf16),
            pltpu.VMEM((4, half, GB, SPAN, depth), f32),
            pltpu.VMEM((2, half, inner_rows, depth), f32),
            pltpu.VMEM((2, half, inner_rows, depth), f32),
            pltpu.VMEM((2, half, outer_rows, depth), f32),
            pltpu.VMEM((2, half, outer_rows, depth), f32),
            pltpu.SemaphoreType.DMA((6,)),
            pltpu.SemaphoreType.DMA((4, 2)),
            pltpu.SemaphoreType.DMA((4, 2)),
            pltpu.SemaphoreType.DMA((4, 2)),
            pltpu.SemaphoreType.DMA((devices,)),
            pltpu.SemaphoreType.DMA((devices,)),
            pltpu.SemaphoreType.DMA((4,)),
            pltpu.SemaphoreType.DMA((4,)),
            pltpu.SemaphoreType.DMA((2, 2)),
            pltpu.SemaphoreType.DMA((2, 2)),
        ],
        compiler_params=pltpu.CompilerParams(
            collective_id=1, has_side_effects=True, vmem_limit_bytes=60 * 1024 * 1024
        ),
        cost_estimate=pl.CostEstimate(
            flops=3 * products, bytes_accessed=4 * tiles * steps * width * depth, transcendentals=0
        ),
    )(nbr_device.T, nbr_index.T, depth_extent, q_rate.reshape(1, depth), src_snap, rcv_snap)


def solution(mesh):
    placed = (P("tile", "tm", None, None), P("tile", "tm", None, None), P(), P(), P(), P("tile"))
    body = paired if mesh.shape["tm"] == 4 else local
    return jax.shard_map(
        body,
        mesh=mesh,
        in_specs=placed,
        out_specs=P(("tile", "tm"), None, None, None),
        check_vma=False,
    )
```

profile of v0, /device:TPU:0, one launch (start us, length us, event | category | flops | bytes accessed | tf_op | source)
XLA Modules:
  0.0 59.7 jit_solution(15343198846861374977)
XLA Ops:
  0.0 56.5 %shard_map.64 = f32[4,8,49,256]{3,2,1,0:T(8,128)} custom-call(s32[2,128]{1,0:T(2,128)} %bitcast.3, s32[2,128]{1,0:T(2,128)} %bitcast.4, s32[16]{0:T(128)} %extent_ref.1, f32[1,256]{1,0:T(1,128)} %bitcast.5, bf16[16,2,128,256]{3,2,1,0:T(8,128)(2,1)} %src_ref.1, bf16[16,2,128,256]{3,2,1,0:T(8,128)(2,1)} %rcv_ref.1), custom_call_target="tpu_custom_call" | custom-call | flops 9633792 | bytes 4194304 | tf_op jit(solution)/shard_map/pallas_call | solution.py:800
  56.5 3.1 %copy.7 = f32[4,8,49,256]{3,1,2,0:T(8,128)} copy(f32[4,8,49,256]{3,2,1,0:T(8,128)} %shard_map.64) | data formatting | bytes 3211264 | tf_op jit(solution)/shard_map/pallas_call | solution.py:800
where the time goes:
time: 59.8 us; the launch traced here: 59.7 us
  Pallas kernels  56.5 us (94%)
  local copies, waits for them, and re-layouts  3.15 us (5%)
    pallas_call x1, Pallas kernels, paired(): pl.pallas_call(functools.partial(pair_kernel, sizes), out_shape=jax.Shape...  56.5 us
    pallas_call x1, local copies, waits for them, and re-layouts, paired(): pl.pallas_call(functools.partial(pair_kernel, sizes), out_shape=jax.Shape...  3.15 us

commit v1 on v0

--- a/solution.py
+++ b/solution.py
@@ -388,13 +388,17 @@
 
 def pair_kernel(
     sizes,
+    device_in,
+    index_in,
+    extent_in,
+    rate_in,
+    src_ref,
+    rcv_ref,
+    out_ref,
     device_tab,
     index_tab,
     extent_ref,
     rate_ref,
-    src_ref,
-    rcv_ref,
-    out_ref,
     ranks,
     edge_cells,
     a_send,
@@ -404,10 +408,12 @@
     b_recv,
     centre,
     acc,
+    turned_out,
     pc_send,
     pc_recv,
     pe_send,
     pe_recv,
+    small_sem,
     edge_sem,
     own_sem,
     main_send_sem,
@@ -439,6 +445,19 @@
     def first_tile(owners, w):
         return owners[w] * share + offset[w]
 
+    barrier = pltpu.get_barrier_semaphore()
+    for to in (by_x, by_y):
+        pl.semaphore_signal(barrier, inc=1, device_id=(me_tile, to), device_id_type=MESH)
+    for j in range(1, devices):
+        pl.semaphore_signal(
+            barrier, inc=1, device_id=(lax.rem(me_tile + j, devices), me_tm), device_id_type=MESH
+        )
+    small_copies = []
+    smalls = ((device_in, device_tab), (index_in, index_tab), (extent_in, extent_ref), (rate_in, rate_ref))
+    for k, (source, target) in enumerate(smalls):
+        copy = pltpu.make_async_copy(source, target, small_sem.at[k])
+        copy.start()
+        small_copies.append(copy)
     edge_copies = []
     for f in range(2):
         for k, first in enumerate((width - ROWS, 0, ROWS)):
@@ -450,17 +469,11 @@
             copy.start()
             edge_copies.append(copy)
 
-    barrier = pltpu.get_barrier_semaphore()
-    for to in (by_x, by_y):
-        pl.semaphore_signal(barrier, inc=1, device_id=(me_tile, to), device_id_type=MESH)
-    for j in range(1, devices):
-        pl.semaphore_signal(
-            barrier, inc=1, device_id=(lax.rem(me_tile + j, devices), me_tm), device_id_type=MESH
-        )
     pl.semaphore_wait(barrier, devices + 1)
 
     main_copies = []
-    for w in range(4):
+
+    def start_main(w):
         copies = []
         for f in range(2):
             copy = pltpu.make_async_remote_copy(
@@ -474,6 +487,9 @@
             copy.start()
             copies.append(copy)
         main_copies.append(copies)
+
+    for w in range(2):
+        start_main(w)
     own_copies = []
     for w in range(4):
         for f in range(2):
@@ -485,7 +501,7 @@
             copy.start()
             own_copies.append(copy)
 
-    for copy in edge_copies:
+    for copy in small_copies + edge_copies:
         copy.wait()
 
     a_extra = a_send.shape[1] - capacity * pieces
@@ -520,8 +536,17 @@
             a_extra, ROWS, depth
         )
 
+    def other(j):
+        total, unit = jnp.int32(0), 1
+        while unit < devices:
+            mine = lax.rem(lax.div(me_tile, unit), 2)
+            flip = lax.rem(lax.div(j, unit), 2)
+            total = total + (mine + flip - 2 * mine * flip) * unit
+            unit *= 2
+        return total
+
     def a_copy(j):
-        to = lax.rem(me_tile + j, devices)
+        to = other(j)
         return pltpu.make_async_remote_copy(
             src_ref=a_send.at[to],
             dst_ref=a_recv.at[me_tile],
@@ -532,10 +557,13 @@
         )
 
     @pl.loop(1, devices)
-    def _(j):
-        pack(lax.rem(me_tile + j, devices))
+    def _(back):
+        j = devices - back
+        pack(other(j))
         a_copy(j).start()
 
+    for w in (2, 3):
+        start_main(w)
     pack(me_tile)
     a_recv[me_tile] = a_send[me_tile]
 
@@ -718,12 +746,21 @@
         @pl.loop(0, half)
         def _(i):
             tile = offset[w] + i
-            extent = extent_ref[me_tm * share + tile]
-            cell = lax.broadcasted_iota(jnp.int32, (1, depth), 1)
-            mask = (cell < extent).astype(jnp.float32)
             for k, g in enumerate(gathers):
                 total = acc[w, i, g][:OFFS] + recv[w - 2, i, OFFS * k : OFFS * (k + 1)]
-                out_ref[tile, g] = total * (1.0 / math.sqrt(steps * times)) * mask
+                for part in range(depth // 128):
+                    turned_out[tile, part, pl.ds(g, OFFS, stride=GB), :] = total[
+                        :, 128 * part : 128 * (part + 1)
+                    ]
+            if gathers != outer:
+                return
+            extent = extent_ref[me_tm * share + tile]
+            cell = lax.broadcasted_iota(jnp.int32, (1, 128), 1)
+            for part in range(depth // 128):
+                mask = (cell + 128 * part < extent).astype(jnp.float32)
+                out_ref[tile, :, 128 * part : 128 * (part + 1)] = (
+                    turned_out[tile, part] * (1.0 / math.sqrt(steps * times)) * mask
+                )
 
     for copy in own_copies:
         copy.wait()
@@ -736,6 +773,8 @@
         copy = partial_copy(w, pc_send, pc_recv, 0)
         copy.start()
         pc_copies.append(copy)
+    for w in (2, 3):
+        far_centre(w)
 
     @pl.loop(1, devices)
     def _(j):
@@ -754,7 +793,7 @@
         )
         copy.start()
         b_copies.append(copy)
-    for w in range(4):
+    for w in range(2):
         unpack(first_tile(owner, w), b_own, w)
         own_edge(w)
 
@@ -765,8 +804,8 @@
         copy.start()
         pe_copies.append(copy)
     for w in (2, 3):
-        far_centre(w)
-    for w in (2, 3):
+        unpack(first_tile(owner, w), b_own, w)
+        own_edge(w)
         far_edge(w)
     for w in (2, 3):
         pc_copies[w - 2].wait_recv()
@@ -797,14 +836,16 @@
     sizes = (tiles, steps, width, depth, devices, times, capacity, share)
     bf16, f32 = jnp.bfloat16, jnp.float32
     products = share * GB * OFFS * depth * steps * times
-    return pl.pallas_call(
+    image = pl.pallas_call(
         functools.partial(pair_kernel, sizes),
-        out_shape=jax.ShapeDtypeStruct((share, GB, OFFS, depth), f32),
-        in_specs=[pl.BlockSpec(memory_space=pltpu.SMEM)] * 3
-        + [pl.BlockSpec(memory_space=pltpu.VMEM)]
-        + [pl.BlockSpec(memory_space=pl.ANY)] * 2,
+        out_shape=jax.ShapeDtypeStruct((share, OFFS * GB, depth), f32),
+        in_specs=[pl.BlockSpec(memory_space=pltpu.HBM)] * 6,
         out_specs=pl.BlockSpec(memory_space=pltpu.VMEM),
         scratch_shapes=[
+            pltpu.SMEM(nbr_device.shape[::-1], jnp.int32),
+            pltpu.SMEM(nbr_index.shape[::-1], jnp.int32),
+            pltpu.SMEM(depth_extent.shape, jnp.int32),
+            pltpu.VMEM((1, depth), f32),
             pltpu.SMEM((2, tiles), jnp.int32),
             pltpu.VMEM((2, 3, tiles, steps, ROWS, depth), bf16),
             pltpu.VMEM((devices, a_blocks, ROWS, depth), bf16),
@@ -814,10 +855,12 @@
             pltpu.VMEM((4, b_blocks, ROWS, depth), bf16),
             pltpu.VMEM((2, 2, 4, half, steps, width, depth), bf16),
             pltpu.VMEM((4, half, GB, SPAN, depth), f32),
+            pltpu.VMEM((share, depth // 128, OFFS * GB, 128), f32),
             pltpu.VMEM((2, half, inner_rows, depth), f32),
             pltpu.VMEM((2, half, inner_rows, depth), f32),
             pltpu.VMEM((2, half, outer_rows, depth), f32),
             pltpu.VMEM((2, half, outer_rows, depth), f32),
+            pltpu.SemaphoreType.DMA((4,)),
             pltpu.SemaphoreType.DMA((6,)),
             pltpu.SemaphoreType.DMA((4, 2)),
             pltpu.SemaphoreType.DMA((4, 2)),
@@ -836,6 +879,7 @@
             flops=3 * products, bytes_accessed=4 * tiles * steps * width * depth, transcendentals=0
         ),
     )(nbr_device.T, nbr_index.T, depth_extent, q_rate.reshape(1, depth), src_snap, rcv_snap)
+    return image.reshape(share, OFFS, GB, depth).transpose(0, 2, 1, 3)
 
 
 def solution(mesh):

time: 59.8 us -> 58.7 us (0.982)
  Pallas kernels: 56.5 us -> 55.9 us
    pallas_call x1 -> x0, local copies, waits for them, and re-layouts: 3.15 us -> none  [paired(): pl.pallas_call(functools.partial(pair_kernel, sizes), out_shape=jax.Shape...]
    unnamed x0 -> x1, local copies, waits for them, and re-layouts: none -> 2.68 us
where the time goes in v1:
time: 58.7 us; the launch traced here: 58.6 us
  Pallas kernels  55.9 us (95%)
  local copies, waits for them, and re-layouts  2.68 us (5%)
    pallas_call x1, Pallas kernels, paired(): pl.pallas_call(functools.partial(pair_kernel, sizes), out_shape=jax.Shape...  55.9 us
    unnamed x1, local copies, waits for them, and re-layouts  2.68 us

profile of v1, /device:TPU:0, one launch (start us, length us, event | category | flops | bytes accessed | tf_op | source)
XLA Modules:
  0.0 58.6 jit_solution(628176419634240042)
XLA Ops:
  0.0 55.9 %shard_map.64 = f32[4,392,256]{2,1,0:T(8,128)} custom-call(s32[2,128]{1,0:T(2,128)} %bitcast.7, s32[2,128]{1,0:T(2,128)} %bitcast.8, s32[16]{0:T(128)} %extent_in.1, f32[1,256]{1,0:T(1,128)} %bitcast.9, bf16[16,2,128,256]{3,2,1,0:T(8,128)(2,1)} %src_ref.1, bf16[16,2,128,256]{3,2,1,0:T(8,128)(2,1)} %rcv_ref.1), custom_call_target="tpu_custom_call" | custom-call | flops 9633792 | bytes 4194304 | tf_op jit(solution)/shard_map/pallas_call | solution.py:839
  55.9 2.7 %copy.8 = f32[4,8,49,256]{3,1,2,0:T(8,128)} copy(f32[4,8,49,256]{3,1,2,0:T(8,128)} %bitcast.6) | data formatting | bytes 3211264

commit v2 on v1

--- a/solution.py
+++ b/solution.py
@@ -408,6 +408,7 @@
     b_recv,
     centre,
     acc,
+    acc_mid,
     turned_out,
     pc_send,
     pc_recv,
@@ -594,22 +595,39 @@
 
     inner = range(1, GB - 2)
     outer = (0, GB - 2, GB - 1)
-    turn_centre = one_hot(
-        width - 8, width, lambda row, column: column == width - ROWS - row
+    middle = ((0, 16, 17, 0), (GB - 2, 1, 47, 25), (GB - 1, 17, 15, 73))
+    border = (
+        (0, 0, 16),
+        (0, 33, 16),
+        (GB - 1, 0, 17),
+        (GB - 1, 32, 17),
+        (GB - 2, 0, 1),
+        (GB - 2, 48, 1),
     )
-    last = width // GSTEP * GSTEP - HMAX * 2
+    turn_centre = one_hot(width + 8, width, lambda row, column: column == width - row)
+    last = width // GSTEP * GSTEP + ROWS - HMAX * 2
 
     def centre_sums(w, p, part, i):
         sums = [None] * GB
+        mids = [None] * 3
         for t in range(steps):
             turned = pick(turn_centre, centre[0, p, w, i, t]) * weight(part, t)
             straight = centre[1, p, w, i, t].astype(jnp.float32)
+            products = (
+                turned[width - ROWS :] * straight[:24],
+                turned[: 3 * ROWS] * straight[width - 3 * ROWS :],
+                turned[:ROWS] * straight[width - ROWS :],
+            )
+            mids = [
+                product if total is None else total + product
+                for total, product in zip(mids, products)
+            ]
             for g in inner:
                 back = last - GSTEP * g
                 ahead = GSTEP * (g - 1)
                 product = turned[back : back + SPAN] * straight[ahead : ahead + SPAN]
                 sums[g] = product if sums[g] is None else sums[g] + product
-        return sums
+        return sums, jnp.concatenate(mids, axis=0)
 
     turn_first = one_hot(SPAN, 4 * ROWS, lambda row, column: column == OFFS - 1 - row)
     turn_last = one_hot(SPAN + ROWS, 4 * ROWS, lambda row, column: column == 4 * ROWS - row)
@@ -672,9 +690,10 @@
     def own_centre(w):
         @pl.loop(0, half)
         def _(i):
-            sums = centre_sums(w, 0, me_tm, i)
+            sums, mids = centre_sums(w, 0, me_tm, i)
             for g in inner:
                 acc[w, i, g] = sums[g]
+            acc_mid[w, i] = mids
 
     def own_edge(w):
         @pl.loop(0, half)
@@ -688,7 +707,15 @@
 
         @pl.loop(0, half)
         def _(i):
-            sums = centre_sums(w, 1, partner[w], i)
+            sums, mids = centre_sums(w, 1, partner[w], i)
+            mids = acc_mid[w, i] + mids
+            if w < 2:
+                first = OFFS * len(inner)
+                for _, _, count, place in middle:
+                    pc_send[w, i, first : first + count] = mids[place : place + count]
+                    first += count
+            else:
+                acc_mid[w, i] = mids
             for k, g in enumerate(inner):
                 total = acc[w, i, g] + sums[g]
                 if w < 2:
@@ -702,12 +729,15 @@
         @pl.loop(0, half)
         def _(i):
             sums = edge_sums(b_recv, w, 1, partner[w], i)
-            for k, g in enumerate(outer):
-                total = acc[w, i, g] + sums[k]
-                if w < 2:
-                    pe_send[w, i, OFFS * k : OFFS * (k + 1)] = total[:OFFS]
-                else:
-                    acc[w, i, g] = total
+            totals = {g: acc[w, i, g] + sums[k] for k, g in enumerate(outer)}
+            if w < 2:
+                first = 0
+                for g, offs, count in border:
+                    pe_send[w, i, first : first + count] = totals[g][offs : offs + count]
+                    first += count
+            else:
+                for g in outer:
+                    acc[w, i, g] = totals[g]
 
     def partial_copy(w, send, recv, k):
         return pltpu.make_async_remote_copy(
@@ -742,18 +772,36 @@
             packed = chosen if packed is None else packed + chosen
         target[w, b_rims:] = packed.astype(jnp.bfloat16).reshape(b_extra, ROWS, depth)
 
-    def finish(w, gathers, recv):
+    def place_rows(tile, g, offs, count, rows):
+        for part in range(depth // 128):
+            turned_out[tile, part, pl.ds(offs * GB + g, count, stride=GB), :] = rows[
+                :, 128 * part : 128 * (part + 1)
+            ]
+
+    def finish_early(w):
         @pl.loop(0, half)
         def _(i):
             tile = offset[w] + i
-            for k, g in enumerate(gathers):
-                total = acc[w, i, g][:OFFS] + recv[w - 2, i, OFFS * k : OFFS * (k + 1)]
-                for part in range(depth // 128):
-                    turned_out[tile, part, pl.ds(g, OFFS, stride=GB), :] = total[
-                        :, 128 * part : 128 * (part + 1)
-                    ]
-            if gathers != outer:
-                return
+            first = 0
+            for g in inner:
+                got = pc_recv[w - 2, i, first : first + OFFS]
+                place_rows(tile, g, 0, OFFS, acc[w, i, g][:OFFS] + got)
+                first += OFFS
+            mids = acc_mid[w, i]
+            for g, offs, count, place in middle:
+                got = pc_recv[w - 2, i, first : first + count]
+                place_rows(tile, g, offs, count, mids[place : place + count] + got)
+                first += count
+
+    def finish_late(w):
+        @pl.loop(0, half)
+        def _(i):
+            tile = offset[w] + i
+            first = 0
+            for g, offs, count in border:
+                got = pe_recv[w - 2, i, first : first + count]
+                place_rows(tile, g, offs, count, acc[w, i, g][offs : offs + count] + got)
+                first += count
             extent = extent_ref[me_tm * share + tile]
             cell = lax.broadcasted_iota(jnp.int32, (1, 128), 1)
             for part in range(depth // 128):
@@ -809,10 +857,10 @@
         far_edge(w)
     for w in (2, 3):
         pc_copies[w - 2].wait_recv()
-        finish(w, inner, pc_recv)
+        finish_early(w)
     for w in (2, 3):
         pe_copies[w - 2].wait_recv()
-        finish(w, outer, pe_recv)
+        finish_late(w)
 
     for copies in main_copies:
         for copy in copies:
@@ -831,8 +879,8 @@
     pieces = 2 * steps
     a_blocks = capacity * pieces + -(-capacity * pieces // ROWS)
     b_blocks = 2 * half * steps * 2 + -(-half * pieces // ROWS)
-    inner_rows = -(-(GB - 3) * OFFS // 8) * 8
-    outer_rows = -(-3 * OFFS // 8) * 8
+    inner_rows = 328
+    outer_rows = 72
     sizes = (tiles, steps, width, depth, devices, times, capacity, share)
     bf16, f32 = jnp.bfloat16, jnp.float32
     products = share * GB * OFFS * depth * steps * times
@@ -855,6 +903,7 @@
             pltpu.VMEM((4, b_blocks, ROWS, depth), bf16),
             pltpu.VMEM((2, 2, 4, half, steps, width, depth), bf16),
             pltpu.VMEM((4, half, GB, SPAN, depth), f32),
+            pltpu.VMEM((4, half, 88, depth), f32),
             pltpu.VMEM((share, depth // 128, OFFS * GB, 128), f32),
             pltpu.VMEM((2, half, inner_rows, depth), f32),
             pltpu.VMEM((2, half, inner_rows, depth), f32),

time: 58.7 us -> 58.6 us (level)
  no operation moved by 1% of the time
where the time goes in v2:
time: 58.6 us; the launch traced here: 58.5 us
  Pallas kernels  55.8 us (95%)
  local copies, waits for them, and re-layouts  2.68 us (5%)
    pallas_call x1, Pallas kernels, paired(): pl.pallas_call(functools.partial(pair_kernel, sizes), out_shape=jax.Shape...  55.8 us
    unnamed x1, local copies, waits for them, and re-layouts  2.68 us

profile of v2, /device:TPU:0, one launch (start us, length us, event | category | flops | bytes accessed | tf_op | source)
XLA Modules:
  0.0 58.5 jit_solution(2341453318750075624)
XLA Ops:
  0.0 55.8 %shard_map.64 = f32[4,392,256]{2,1,0:T(8,128)} custom-call(s32[2,128]{1,0:T(2,128)} %bitcast.7, s32[2,128]{1,0:T(2,128)} %bitcast.8, s32[16]{0:T(128)} %extent_in.1, f32[1,256]{1,0:T(1,128)} %bitcast.9, bf16[16,2,128,256]{3,2,1,0:T(8,128)(2,1)} %src_ref.1, bf16[16,2,128,256]{3,2,1,0:T(8,128)(2,1)} %rcv_ref.1), custom_call_target="tpu_custom_call" | custom-call | flops 9633792 | bytes 4194304 | tf_op jit(solution)/shard_map/pallas_call | solution.py:887
  55.8 2.7 %copy.8 = f32[4,8,49,256]{3,1,2,0:T(8,128)} copy(f32[4,8,49,256]{3,1,2,0:T(8,128)} %bitcast.6) | data formatting | bytes 3211264

commit v3 on v2

--- a/solution.py
+++ b/solution.py
@@ -409,6 +409,8 @@
     centre,
     acc,
     acc_mid,
+    acc_edge,
+    kept,
     turned_out,
     pc_send,
     pc_recv,
@@ -593,25 +595,33 @@
         step = (part * steps + t).astype(jnp.float32)
         return jnp.exp(rate * step / (steps * times))
 
+    weights = [[weight(part, t) for t in range(steps)] for part in (me_tm, by_x, by_y)]
+
+    def weights_of(p, w):
+        return weights[0] if p == 0 else weights[1 + w % 2]
+
     inner = range(1, GB - 2)
-    outer = (0, GB - 2, GB - 1)
     middle = ((0, 16, 17, 0), (GB - 2, 1, 47, 25), (GB - 1, 17, 15, 73))
     border = (
         (0, 0, 16),
         (0, 33, 16),
-        (GB - 1, 0, 17),
-        (GB - 1, 32, 17),
+        (GB - 1, 1, 16),
+        (GB - 1, 32, 16),
+        (GB - 1, 0, 1),
+        (GB - 1, 48, 1),
         (GB - 2, 0, 1),
         (GB - 2, 48, 1),
     )
     turn_centre = one_hot(width + 8, width, lambda row, column: column == width - row)
     last = width // GSTEP * GSTEP + ROWS - HMAX * 2
 
-    def centre_sums(w, p, part, i):
+    def centre_sums(w, p, i):
         sums = [None] * GB
         mids = [None] * 3
         for t in range(steps):
-            turned = pick(turn_centre, centre[0, p, w, i, t]) * weight(part, t)
+            turned = pick(turn_centre, centre[0, p, w, i, t]) * weights_of(p, w)[t]
+            kept[p, w, i, t, : 3 * ROWS] = turned[ROWS : 4 * ROWS]
+            kept[p, w, i, t, 3 * ROWS :] = turned[6 * ROWS : 7 * ROWS]
             straight = centre[1, p, w, i, t].astype(jnp.float32)
             products = (
                 turned[width - ROWS :] * straight[:24],
@@ -629,77 +639,64 @@
                 sums[g] = product if sums[g] is None else sums[g] + product
         return sums, jnp.concatenate(mids, axis=0)
 
-    turn_first = one_hot(SPAN, 4 * ROWS, lambda row, column: column == OFFS - 1 - row)
-    turn_last = one_hot(SPAN + ROWS, 4 * ROWS, lambda row, column: column == 4 * ROWS - row)
-    wide = width - 3 * ROWS
     b_rims = 2 * half * steps * 2
     b_extra = b_send.shape[1] - b_rims
-
-    def edge_sums(rims_ref, w, p, part, i):
-        extra = rims_ref[w, b_rims:].reshape(b_extra * ROWS, depth)
-        sums = [None] * 3
-        for t in range(steps):
-            scale = weight(part, t)
-            place = i * pieces + t
-            rims = (i * steps + t) * 2
-            rims_rcv = ((half + i) * steps + t) * 2
-            turned = pick(
-                turn_first,
-                jnp.concatenate([rims_ref[w, rims], centre[0, p, w, i, t, : 3 * ROWS]], axis=0),
-            )
-            straight = jnp.concatenate(
-                [rims_ref[w, rims_rcv], centre[1, p, w, i, t, : 3 * ROWS]], axis=0
-            ).astype(jnp.float32)
-            products = [turned * scale * straight[:SPAN]]
-            turn_extra = one_hot(
-                SPAN + ROWS,
-                b_extra * ROWS,
-                lambda row, column: (row == 0) & (column == place),
-            )
-            turned = pick(
-                turn_last,
-                jnp.concatenate(
-                    [centre[0, p, w, i, t, wide:], rims_ref[w, rims + 1]], axis=0
-                ),
-            ) + pick(turn_extra, extra)
-            turned = turned * scale
-            rcv_extra = pick(
-                one_hot(
-                    8,
-                    b_extra * ROWS,
-                    lambda row, column: (row == 0) & (column == place + steps),
-                ),
-                extra,
-            )
-            straight = jnp.concatenate(
-                [
-                    centre[1, p, w, i, t, wide:].astype(jnp.float32),
-                    rims_ref[w, rims_rcv + 1].astype(jnp.float32),
-                    rcv_extra,
-                ],
-                axis=0,
-            )
-            products.append(turned[ROWS:] * straight[:SPAN])
-            products.append(turned[:SPAN] * straight[ROWS:])
-            sums = [
-                product if total is None else total + product
-                for total, product in zip(sums, products)
-            ]
-        return sums
+    rim_rows = b_rims // 2 * ROWS
+    turn_rims = one_hot(
+        rim_rows,
+        rim_rows,
+        lambda row, column: column == row // ROWS * (2 * ROWS) + ROWS - 1 - row,
+    )
+
+    def edge_sums(rims_ref, w, p):
+        extra = rims_ref[w, b_rims:].reshape(b_extra * ROWS, depth).astype(jnp.float32)
+        turned_rims = pick(turn_rims, rims_ref[w, : b_rims // 2].reshape(rim_rows, depth))
+        found = []
+        for i in range(half):
+            total = None
+            for t in range(steps):
+                scale = weights_of(p, w)[t]
+                place = i * pieces + t
+                block = (i * steps + t) * 2
+                left = turned_rims[block * ROWS : (block + 1) * ROWS] * scale
+                right = turned_rims[(block + 1) * ROWS : (block + 2) * ROWS] * scale
+                rims_rcv = b_rims // 2 + block
+                rcv_left = rims_ref[w, rims_rcv].astype(jnp.float32)
+                rcv_right = rims_ref[w, rims_rcv + 1].astype(jnp.float32)
+                turned = kept[p, w, i, t]
+                near = centre[1, p, w, i, t, ROWS : 3 * ROWS].astype(jnp.float32)
+                far = centre[1, p, w, i, t, width - 3 * ROWS :].astype(jnp.float32)
+                src_extra = extra[place : place + 1] * scale
+                rcv_extra = extra[place + steps : place + steps + 1]
+                product = jnp.concatenate(
+                    [
+                        turned[3 * ROWS :] * rcv_left,
+                        left * near[1 : ROWS + 1],
+                        right * far[ROWS + 1 : 2 * ROWS + 1],
+                        turned[:ROWS] * rcv_right,
+                        src_extra * far[ROWS : ROWS + 1],
+                        turned[ROWS : ROWS + 1] * rcv_extra,
+                        right[ROWS - 1 :] * far[:1],
+                        turned[2 * ROWS : 2 * ROWS + 1] * rcv_right[:1],
+                        jnp.zeros((4, depth), jnp.float32),
+                    ],
+                    axis=0,
+                )
+                total = product if total is None else total + product
+            found.append(total)
+        return found
 
     def own_centre(w):
         @pl.loop(0, half)
         def _(i):
-            sums, mids = centre_sums(w, 0, me_tm, i)
+            sums, mids = centre_sums(w, 0, i)
             for g in inner:
                 acc[w, i, g] = sums[g]
             acc_mid[w, i] = mids
 
     def own_edge(w):
-        @pl.loop(0, half)
-        def _(i):
-            for g, total in zip(outer, edge_sums(b_own, w, 0, me_tm, i)):
-                acc[w, i, g] = total
+        for i, total in enumerate(edge_sums(b_own, w, 0)):
+            acc_edge[w, i] = total
 
     def far_centre(w):
         for copy in main_copies[w]:
@@ -707,7 +704,7 @@
 
         @pl.loop(0, half)
         def _(i):
-            sums, mids = centre_sums(w, 1, partner[w], i)
+            sums, mids = centre_sums(w, 1, i)
             mids = acc_mid[w, i] + mids
             if w < 2:
                 first = OFFS * len(inner)
@@ -725,19 +722,9 @@
 
     def far_edge(w):
         b_copies[w].wait_recv()
-
-        @pl.loop(0, half)
-        def _(i):
-            sums = edge_sums(b_recv, w, 1, partner[w], i)
-            totals = {g: acc[w, i, g] + sums[k] for k, g in enumerate(outer)}
-            if w < 2:
-                first = 0
-                for g, offs, count in border:
-                    pe_send[w, i, first : first + count] = totals[g][offs : offs + count]
-                    first += count
-            else:
-                for g in outer:
-                    acc[w, i, g] = totals[g]
+        target = pe_send if w < 2 else acc_edge
+        for i, total in enumerate(edge_sums(b_recv, w, 1)):
+            target[w, i] = acc_edge[w, i] + total
 
     def partial_copy(w, send, recv, k):
         return pltpu.make_async_remote_copy(
@@ -750,7 +737,10 @@
         )
 
     def unpack(first, target, w):
-        packed = None
+        row = lax.broadcasted_iota(jnp.int32, (b_extra * ROWS, half * a_extra * ROWS), 0)
+        column = lax.broadcasted_iota(jnp.int32, (b_extra * ROWS, half * a_extra * ROWS), 1)
+        chosen = jnp.full(row.shape, False)
+        extras = []
         for i in range(half):
             tile = first + i
             for side in range(2):
@@ -760,16 +750,17 @@
                 for f in range(2):
                     for t in range(steps):
                         target[w, ((f * half + i) * steps + t) * 2 + side] = rim[f * steps + t]
-            extra = a_recv[source, capacity * pieces :].reshape(a_extra * ROWS, depth)
-            choose = one_hot(
-                b_extra * ROWS,
-                a_extra * ROWS,
-                lambda row, column: (row >= i * pieces)
+            extras.append(
+                a_recv[source, capacity * pieces :].reshape(a_extra * ROWS, depth)
+            )
+            chosen = chosen | (
+                (row >= i * pieces)
                 & (row < (i + 1) * pieces)
-                & (column == rank * pieces + row - i * pieces),
+                & (column == i * a_extra * ROWS + rank * pieces + row - i * pieces)
             )
-            chosen = pick(choose, extra)
-            packed = chosen if packed is None else packed + chosen
+        packed = pick(
+            chosen.astype(jnp.float32).astype(jnp.bfloat16), jnp.concatenate(extras, axis=0)
+        )
         target[w, b_rims:] = packed.astype(jnp.bfloat16).reshape(b_extra, ROWS, depth)
 
     def place_rows(tile, g, offs, count, rows):
@@ -800,7 +791,7 @@
             first = 0
             for g, offs, count in border:
                 got = pe_recv[w - 2, i, first : first + count]
-                place_rows(tile, g, offs, count, acc[w, i, g][offs : offs + count] + got)
+                place_rows(tile, g, offs, count, acc_edge[w, i, first : first + count] + got)
                 first += count
             extent = extent_ref[me_tm * share + tile]
             cell = lax.broadcasted_iota(jnp.int32, (1, 128), 1)
@@ -904,6 +895,8 @@
             pltpu.VMEM((2, 2, 4, half, steps, width, depth), bf16),
             pltpu.VMEM((4, half, GB, SPAN, depth), f32),
             pltpu.VMEM((4, half, 88, depth), f32),
+            pltpu.VMEM((4, half, outer_rows, depth), f32),
+            pltpu.VMEM((2, 4, half, steps, 4 * ROWS, depth), f32),
             pltpu.VMEM((share, depth // 128, OFFS * GB, 128), f32),
             pltpu.VMEM((2, half, inner_rows, depth), f32),
             pltpu.VMEM((2, half, inner_rows, depth), f32),

time: 58.6 us -> 58.6 us (level)
  no operation moved by 1% of the time
where the time goes in v3:
time: 58.6 us; the launch traced here: 58.5 us
  Pallas kernels  55.8 us (95%)
  local copies, waits for them, and re-layouts  2.68 us (5%)
    pallas_call x1, Pallas kernels, paired(): pl.pallas_call(functools.partial(pair_kernel, sizes), out_shape=jax.Shape...  55.8 us
    unnamed x1, local copies, waits for them, and re-layouts  2.68 us

profile of v3, /device:TPU:0, one launch (start us, length us, event | category | flops | bytes accessed | tf_op | source)
XLA Modules:
  0.0 58.5 jit_solution(10220456190684816409)
XLA Ops:
  0.0 55.8 %shard_map.64 = f32[4,392,256]{2,1,0:T(8,128)} custom-call(s32[2,128]{1,0:T(2,128)} %bitcast.7, s32[2,128]{1,0:T(2,128)} %bitcast.8, s32[16]{0:T(128)} %extent_in.1, f32[1,256]{1,0:T(1,128)} %bitcast.9, bf16[16,2,128,256]{3,2,1,0:T(8,128)(2,1)} %src_ref.1, bf16[16,2,128,256]{3,2,1,0:T(8,128)(2,1)} %rcv_ref.1), custom_call_target="tpu_custom_call" | custom-call | flops 9633792 | bytes 4194304 | tf_op jit(solution)/shard_map/pallas_call | solution.py:878
  55.8 2.7 %copy.8 = f32[4,8,49,256]{3,1,2,0:T(8,128)} copy(f32[4,8,49,256]{3,1,2,0:T(8,128)} %bitcast.6) | data formatting | bytes 3211264

commit v4 on v3

--- a/solution.py
+++ b/solution.py
@@ -820,7 +820,8 @@
         a_copy(j).wait()
 
     b_copies = []
-    for w in range(4):
+
+    def send_rims(w):
         unpack(first_tile(owner_there, w), b_send, w)
         copy = pltpu.make_async_remote_copy(
             src_ref=b_send.at[w],
@@ -832,9 +833,14 @@
         )
         copy.start()
         b_copies.append(copy)
+
+    for w in range(2):
+        send_rims(w)
     for w in range(2):
         unpack(first_tile(owner, w), b_own, w)
         own_edge(w)
+    for w in (2, 3):
+        send_rims(w)
 
     pe_copies = []
     for w in range(2):

time: 58.6 us -> 58.6 us (level)
  no operation moved by 1% of the time
where the time goes in v4:
time: 58.6 us; the launch traced here: 58.5 us
  Pallas kernels  55.8 us (95%)
  local copies, waits for them, and re-layouts  2.68 us (5%)
    pallas_call x1, Pallas kernels, paired(): pl.pallas_call(functools.partial(pair_kernel, sizes), out_shape=jax.Shape...  55.8 us
    unnamed x1, local copies, waits for them, and re-layouts  2.68 us

profile of v4, /device:TPU:0, one launch (start us, length us, event | category | flops | bytes accessed | tf_op | source)
XLA Modules:
  0.0 58.5 jit_solution(3932483942996337030)
XLA Ops:
  0.0 55.8 %shard_map.64 = f32[4,392,256]{2,1,0:T(8,128)} custom-call(s32[2,128]{1,0:T(2,128)} %bitcast.7, s32[2,128]{1,0:T(2,128)} %bitcast.8, s32[16]{0:T(128)} %extent_in.1, f32[1,256]{1,0:T(1,128)} %bitcast.9, bf16[16,2,128,256]{3,2,1,0:T(8,128)(2,1)} %src_ref.1, bf16[16,2,128,256]{3,2,1,0:T(8,128)(2,1)} %rcv_ref.1), custom_call_target="tpu_custom_call" | custom-call | flops 9633792 | bytes 4194304 | tf_op jit(solution)/shard_map/pallas_call | solution.py:884
  55.8 2.7 %copy.8 = f32[4,8,49,256]{3,1,2,0:T(8,128)} copy(f32[4,8,49,256]{3,1,2,0:T(8,128)} %bitcast.6) | data formatting | bytes 3211264
